TPU v7x, 32 devices: a whole 2x2x4 slice. The times are simulated.
32 devices in a mesh: space: 8 (over z, y), chan: 4 (over x, core).
Axes of the slice: x: 2, y: 2, z: 4, core: 2. Of those that a mesh axis runs over, the one named last changes fastest.
Arguments:
- latent: bfloat16 [1, 8, 160, 512], P(None, 'space', None, 'chan'), may hold values from -12 to 12
- cache_mid: bfloat16 [2, 8, 160, 512], P(None, 'space', None, 'chan'), may hold values from -6 to 6
- norm1_gain: float32 [512], P('chan'), may hold values from 0.1 to 1.9
- norm1_bias: float32 [512], P('chan'), may hold values from -3 to 3
- conv1_weight: bfloat16 [3, 3, 3, 512, 512], P(None, None, None, 'chan'), may hold values from -0.0625 to 0.0625
- conv1_bias: float32 [512], P('chan'), may hold values from -2 to 2
- cache_up: bfloat16 [2, 16, 320, 512], P(None, 'space', 'chan'), may hold values from -6 to 6
- norm2_gain: float32 [512], replicated, may hold values from 0.1 to 1.9
- norm2_bias: float32 [512], replicated, may hold values from -3 to 3
- conv2_weight: bfloat16 [3, 3, 3, 512, 512], P(None, None, None, None, 'chan'), may hold values from -0.0546875 to 0.0546875
- conv2_bias: float32 [512], replicated, may hold values from -2 to 2
Outputs:
- up_features: bfloat16 [1, 16, 320, 512], P(None, 'space', 'chan')
All inputs are finite; a program needn't handle non-finite values.
Results may differ from a plain program's by a relative error of at most 0.0038.
The roundings to bfloat16 on the way count: a program that leaves them out, or rounds other values in their place, can miss the bound.
Values may be sent and summed in bfloat16 or wider, within the bound.
A program may use at most 64 MiB of HBM per device.

v0:
```python
import jax
import jax.numpy as jnp
from jax import lax
from jax.sharding import PartitionSpec as P

GROUPS = 32
GS = 16


epsilon = 1e-06


def extended(cells, sides, width):
    for axis, dim in sides:
        count = lax.axis_size(axis)
        ends = count - 1
        head = lax.slice_in_dim(cells, 0, width, axis=dim)
        tail = lax.slice_in_dim(cells, cells.shape[dim] - width, cells.shape[dim], axis=dim)
        cells = jnp.concatenate(
            [
                lax.ppermute(tail, axis, [(i, (i + 1) % count) for i in range(ends)]),
                cells,
                lax.ppermute(head, axis, [((i + 1) % count, i) for i in range(ends)]),
            ],
            axis=dim,
        )
    return cells


def unfold(padded, frames, height, breadth):
    pieces = []
    for shift_time in range(3):
        for shift_row in range(3):
            for shift_col in range(3):
                pieces.append(
                    padded[
                        shift_time : shift_time + frames,
                        shift_row : shift_row + height,
                        shift_col : shift_col + breadth,
                        :,
                    ]
                )
    return jnp.concatenate(pieces, axis=-1)


def norm_apply(upsampled, mean_chan, scale_chan, gain, bias):
    scaled = (upsampled.astype(jnp.float32) - mean_chan) * scale_chan
    return jax.nn.silu(scaled * gain + bias).astype(jnp.bfloat16)


def on_device(
    latent,
    cache_mid,
    norm1_gain,
    norm1_bias,
    conv1_weight,
    conv1_bias,
    cache_up,
    norm2_gain,
    norm2_bias,
    conv2_weight,
    conv2_bias,
):
    frames, height, breadth, chan_here = latent.shape
    groups_here = chan_here // GS
    values = latent.astype(jnp.float32)
    grouped = values.reshape(frames, height, breadth, groups_here, GS)
    entries = frames * height * lax.axis_size("space") * breadth * GS
    group_mean = lax.psum(jnp.sum(grouped, axis=(0, 1, 2, 4)), "space") / entries
    centred = grouped - group_mean[:, None]
    group_var = lax.psum(jnp.sum(centred * centred, axis=(0, 1, 2, 4)), "space") / entries
    scaled = (centred * lax.rsqrt(group_var + epsilon)[:, None]).reshape(
        frames, height, breadth, chan_here
    )
    normed_mid = jax.nn.silu(scaled * norm1_gain + norm1_bias).astype(jnp.bfloat16)
    joined = jnp.concatenate([cache_mid, normed_mid], axis=0)
    rimmed = extended(joined, (("space", 1),), 1)
    padded = jnp.pad(rimmed, ((0, 0), (0, 0), (1, 1), (0, 0)))
    columns = unfold(padded, frames, height, breadth).reshape(frames * height * breadth, -1)
    kernel = conv1_weight.reshape(-1, conv1_weight.shape[-1])
    summed = lax.psum_scatter(
        lax.dot_general(
            kernel, columns, (((0,), (1,)), ((), ())), preferred_element_type=jnp.float32
        ),
        "chan",
        scatter_dimension=0,
        tiled=True,
    )
    conv_mid = summed.T.reshape(frames, height, breadth, chan_here)
    merged = (values + conv_mid + conv1_bias).astype(jnp.bfloat16)
    merged_groups = merged.astype(jnp.float32).reshape(frames, height, breadth, groups_here, GS)
    first_group = lax.axis_index("chan") * groups_here

    def place(partial_value):
        return lax.dynamic_update_slice_in_dim(
            jnp.zeros((GROUPS,), jnp.float32), partial_value, first_group, 0
        )

    own_sum = jnp.sum(merged_groups, axis=(0, 1, 2, 4))
    group_sums, group_squares = lax.psum(
        (place(own_sum), place(jnp.sum(merged_groups * merged_groups, axis=(0, 1, 2, 4)))),
        ("space", "chan"),
    )
    up_mean = group_sums / entries
    up_var = group_squares / entries - up_mean * up_mean
    mean_chan = jnp.repeat(up_mean, GS)
    scale_chan = jnp.repeat(lax.rsqrt(up_var + epsilon), GS)
    pixel_tile = lax.all_to_all(merged, "chan", split_axis=2, concat_axis=3, tiled=True)
    upsampled = jnp.repeat(jnp.repeat(pixel_tile, 2, axis=1), 2, axis=2)
    normed_up = norm_apply(upsampled, mean_chan, scale_chan, norm2_gain, norm2_bias)
    joined_up = jnp.concatenate([cache_up, normed_up], axis=0)
    rimmed_up = extended(joined_up, (("space", 1), ("chan", 2)), 1)
    up_height = normed_up.shape[1]
    up_breadth = normed_up.shape[2]
    up_columns = unfold(rimmed_up, frames, up_height, up_breadth).reshape(
        frames * up_height * up_breadth, -1
    )
    kernel_up = conv2_weight.reshape(-1, conv2_weight.shape[-1])
    up_conv = jnp.dot(
        up_columns,
        lax.all_gather(kernel_up, "chan", axis=1, tiled=True),
        preferred_element_type=jnp.float32,
    )
    result = (up_conv + conv2_bias).astype(jnp.bfloat16).reshape(frames, up_height, up_breadth, -1)
    return result


def solution(mesh):
    placed = (
        P(None, "space", None, "chan"),
        P(None, "space", None, "chan"),
        P("chan"),
        P("chan"),
        P(None, None, None, "chan", None),
        P("chan"),
        P(None, "space", "chan", None),
        P(),
        P(),
        P(None, None, None, None, "chan"),
        P(),
    )
    return jax.shard_map(
        on_device,
        mesh=mesh,
        in_specs=placed,
        out_specs=P(None, "space", "chan", None),
        check_vma=False,
    )
```

profile of v0, /device:TPU:9, one launch (start us, length us, event | category | flops | bytes accessed | tf_op | source)
XLA Modules:
  0.0 209.5 jit_solution(13262604118124301)
XLA Ops:
  6.5 1.0 convert_reduce_fusion
  7.7 15.1 %psum.28 = f32[8]{0:T(128)S(1)} all-reduce(f32[8]{0:T(128)S(1)} %reduce_sum.51), channel_id=1, replica_groups=mesh['space'=8,'chan'=4] {'space'}, use_global_device_ids=true, to_apply=%region_2.0 | all-reduce | flops 8 | bytes 64 | tf_op jit(solution)/shard_map/psum | solution.py:69
  24.0 13.7 %psum.29 = f32[8]{0:T(128)S(1)} all-reduce(f32[8]{0:T(128)S(1)} %reduce_sum.54), channel_id=1, replica_groups=mesh['space'=8,'chan'=4] {'space'}, use_global_device_ids=true, to_apply=%region_5.6 | all-reduce | flops 8 | bytes 64 | tf_op jit(solution)/shard_map/psum | solution.py:71
  38.7 0.9 pad_maximum_fusion.10
  39.6 3.7 %collective-permute-start = (bf16[3,1,160,128]{3,2,1,0:T(8,128)(2,1)S(1)}, bf16[3,1,160,128]{3,2,1,0:T(8,128)(2,1)S(1)}, u32[]{:S(2)}, u32[]{:S(2)}) collective-permute-start(bf16[3,1,160,128]{3,2,1,0:T(8,128)(2,1)S(1)} %pad_maximum_fusion.10), channel_id=1, source_target_pairs={{0,4},{4,8},{8,12},{12,16},{16,20},{20,24},{24,28},{1,5},{5,9},{9,... | collective-permute-start | bytes 368648 | tf_op jit(solution)/shard_map/ppermute | solution.py:21
  43.3 4.3 %collective-permute-start.1 = (bf16[3,1,160,128]{3,2,1,0:T(8,128)(2,1)S(1)}, bf16[3,1,160,128]{3,2,1,0:T(8,128)(2,1)S(1)}, u32[]{:S(2)}, u32[]{:S(2)}) collective-permute-start(bf16[3,1,160,128]{3,2,1,0:T(8,128)(2,1)S(1)} %pad_maximum_fusion.10), channel_id=1, source_target_pairs={{4,0},{8,4},{12,8},{16,12},{20,16},{24,20},{28,24},{5,1},{9,5},{13... | collective-permute-start | bytes 368648 | tf_op jit(solution)/shard_map/ppermute | solution.py:23
  48.0 1.5 collective-permute-done.1
  49.5 1.0 select_maximum_fusion
  52.0 1.5 convolution_bitcast_fusion
  54.2 28.3 %reduce-scatter.2.cloned.1.call-done = f32[128,160]{0,1:T(8,128)} async-done(((f32[512,160]{0,1:T(8,128)}), f32[128,160]{0,1:T(8,128)}) %reduce-scatter.2.cloned.1.call-update) | async-done | bytes 81936 | tf_op jit(solution)/shard_map/reduce_scatter | solution.py:81
  82.5 0.9 convert_reduce_fusion.1
  84.7 2.3 %reduce.10 = bf16[160,128]{1,0:T(8,128)(2,1)} reduce(bf16[160,1,1,128]{3,2,1,0:T(2,128)(2,1)} %bitcast.86, bf16[]{:T(256)} %broadcast.167), dimensions={1,2}, to_apply=%bitcast.53.reduce_sub_computation | reduce | bytes 81922
  87.0 1.4 reshape.193
  89.2 4.6 %all-to-all-start = ((bf16[4,2,2560]{2,1,0:T(2,128)(2,1)}), bf16[4,2,2560]{2,1,0:T(2,128)(2,1)}, u32[]{:S(2)}, u32[]{:S(2)}) async-start(bf16[4,2,2560]{2,1,0:T(2,128)(2,1)} %reshape.193), calls=%async_computation.1 | async-start | bytes 81920 | tf_op jit(solution)/shard_map/all_to_all | solution.py:108
  93.8 40.6 %all-reduce.1 = (f32[32]{0:T(128)S(1)}, f32[32]{0:T(128)S(1)}) all-reduce(f32[32]{0:T(128)S(1)} %dynamic_update_slice.7, f32[32]{0:T(128)S(1)} %dynamic_update_slice.6), channel_id=1, replica_groups=mesh['space'=8,'chan'=4] {'space','chan'}, use_global_device_ids=true, to_apply=%region_12.13 | all-reduce | flops 64 | bytes 512 | tf_op jit(solution)/shard_map/psum | solution.py:100
  137.0 1.4 reshape.194
  138.4 1.0 bitcast_convert_fusion
  140.8 1.7 convert_element_type.67
  142.5 1.0 multiply_convert_fusion.1
  144.2 1.8 fusion.6
  146.0 2.2 %collective-permute-start.2 = (bf16[3,1,80,512]{3,2,1,0:T(8,128)(2,1)}, bf16[3,1,80,512]{3,2,1,0:T(8,128)(2,1)}, u32[]{:S(2)}, u32[]{:S(2)}) collective-permute-start(bf16[3,1,80,512]{3,2,1,0:T(8,128)(2,1)} %get-tuple-element.41), channel_id=1, source_target_pairs={{0,4},{4,8},{8,12},{12,16},{16,20},{20,24},{24,28},{1,5},{5,9},{9,... | collective-permute-start | bytes 737288 | tf_op jit(solution)/shard_map/ppermute | solution.py:21
  148.3 4.0 %collective-permute-start.3 = (bf16[3,1,80,512]{3,2,1,0:T(8,128)(2,1)}, bf16[3,1,80,512]{3,2,1,0:T(8,128)(2,1)}, u32[]{:S(2)}, u32[]{:S(2)}) collective-permute-start(bf16[3,1,80,512]{3,2,1,0:T(8,128)(2,1)} %get-tuple-element.42), channel_id=1, source_target_pairs={{4,0},{8,4},{12,8},{16,12},{20,16},{24,20},{28,24},{5,1},{9,5},{13... | collective-permute-start | bytes 737288 | tf_op jit(solution)/shard_map/ppermute | solution.py:23
  152.2 1.7 broadcast_in_dim.24
  153.9 1.9 convert_element_type.70
  156.1 6.2 %collective-permute-done.3 = bf16[3,1,80,512]{3,2,1,0:T(8,128)(2,1)} collective-permute-done((bf16[3,1,80,512]{3,2,1,0:T(8,128)(2,1)}, bf16[3,1,80,512]{3,2,1,0:T(8,128)(2,1)}, u32[]{:S(2)}, u32[]{:S(2)}) %collective-permute-start.3) | collective-permute-done | bytes 245792 | tf_op jit(solution)/shard_map/ppermute | solution.py:23
  162.3 0.9 pad_maximum_fusion.11
  163.2 2.5 %collective-permute-start.4 = (bf16[3,4,1,512]{3,2,1,0:T(2,128)(2,1)S(1)}, bf16[3,4,1,512]{3,2,1,0:T(2,128)(2,1)S(1)}, u32[]{:S(2)}, u32[]{:S(2)}) collective-permute-start(bf16[3,4,1,512]{3,2,1,0:T(2,128)(2,1)S(1)} %get-tuple-element.31), channel_id=1, source_target_pairs={{0,1},{1,2},{2,3},{4,5},{5,6},{6,7},{8,9},{9,10},{10,11},{12,13},{... | collective-permute-start | bytes 36872 | tf_op jit(solution)/shard_map/ppermute | solution.py:21
  165.8 1.9 collective-permute-start.5
  167.7 1.4 pad_maximum_fusion.2
  169.1 2.7 %collective-permute-done.5 = bf16[3,4,1,512]{3,2,1,0:T(2,128)(2,1)S(1)} collective-permute-done((bf16[3,4,1,512]{3,2,1,0:T(2,128)(2,1)S(1)}, bf16[3,4,1,512]{3,2,1,0:T(2,128)(2,1)S(1)}, u32[]{:S(2)}, u32[]{:S(2)}) %collective-permute-start.5) | collective-permute-done | bytes 12320 | tf_op jit(solution)/shard_map/ppermute | solution.py:23
  171.8 1.8 pad_maximum_fusion
  193.2 9.5 %fusion = bf16[160,512]{1,0:T(8,128)(2,1)} fusion(bf16[160,13824]{1,0:T(8,128)(2,1)} %constant_dynamic-update-slice_fusion.27, bf16[13824,512]{1,0:T(8,128)(2,1)} %all-gather.2.cloned.1.call-done, f32[512]{0:T(512)S(1)} %copy-done.12), kind=kOutput, calls=%fused_computation.2 | convolution fusion | flops 2265088000 | bytes 18745344 | tf_op jit(solution)/shard_map/dot_general | solution.py:119
  (128 shorter events, 31.3 us)
Async XLA Ops:
  6.5 45.4 %copy-start = (bf16[3,3,3,128,512]{4,3,2,1,0:T(8,128)(2,1)S(1)}, bf16[3,3,3,128,512]{4,3,2,1,0:T(8,128)(2,1)}, u32[]{:S(2)}) copy-start(bf16[3,3,3,128,512]{4,3,2,1,0:T(8,128)(2,1)} %param.15) | copy-start | bytes 10616836
  6.5 45.2 %copy-start.13 = (f32[128]{0:T(128)S(1)}, f32[128]{0:T(128)}, u32[]{:S(2)}) copy-start(f32[128]{0:T(128)} %param.14) | copy-start | bytes 1540
  6.5 76.0 %reduce-scatter.2.cloned.1.call-start = ((), (), s32[]{:S(2)}) async-start(), calls=%async_computation.2 | async-start | bytes 409600 | tf_op jit(solution)/shard_map/reduce_scatter | solution.py:81
  37.8 13.7 %copy-start.6 = (bf16[2,1,160,128]{3,2,1,0:T(8,128)(2,1)S(1)}, bf16[2,1,160,128]{3,2,1,0:T(8,128)(2,1)}, u32[]{:S(2)}) copy-start(bf16[2,1,160,128]{3,2,1,0:T(8,128)(2,1)} %param.12) | copy-start | bytes 245764
  37.8 14.0 %copy-start.5 = (bf16[1,1,160,128]{3,2,1,0:T(8,128)(2,1)S(1)}, bf16[1,1,160,128]{3,2,1,0:T(8,128)(2,1)}, u32[]{:S(2)}) copy-start(bf16[1,1,160,128]{3,2,1,0:T(8,128)(2,1)} %param.11) | copy-start | bytes 122884
  37.8 14.0 %copy-start.14 = (f32[128]{0:T(128)S(1)}, f32[128]{0:T(128)}, u32[]{:S(2)}) copy-start(f32[128]{0:T(128)} %param.13) | copy-start | bytes 1540
  39.6 8.4 %collective-permute-start = (bf16[3,1,160,128]{3,2,1,0:T(8,128)(2,1)S(1)}, bf16[3,1,160,128]{3,2,1,0:T(8,128)(2,1)S(1)}, u32[]{:S(2)}, u32[]{:S(2)}) collective-permute-start(bf16[3,1,160,128]{3,2,1,0:T(8,128)(2,1)S(1)} %pad_maximum_fusion.10), channel_id=1, source_target_pairs={{0,4},{4,8},{8,12},{12,16},{16,20},{20,24},{24,28},{1,5},{5,9},{9,... | collective-permute-start | bytes 368648 | tf_op jit(solution)/shard_map/ppermute | solution.py:21
  43.3 6.2 %collective-permute-start.1 = (bf16[3,1,160,128]{3,2,1,0:T(8,128)(2,1)S(1)}, bf16[3,1,160,128]{3,2,1,0:T(8,128)(2,1)S(1)}, u32[]{:S(2)}, u32[]{:S(2)}) collective-permute-start(bf16[3,1,160,128]{3,2,1,0:T(8,128)(2,1)S(1)} %pad_maximum_fusion.10), channel_id=1, source_target_pairs={{4,0},{8,4},{12,8},{16,12},{20,16},{24,20},{28,24},{5,1},{9,5},{13... | collective-permute-start | bytes 368648 | tf_op jit(solution)/shard_map/ppermute | solution.py:23
  53.4 29.1 %copy-start.15 = (f32[128]{0:T(128)S(1)}, f32[128]{0:T(128)}, u32[]{:S(2)}) copy-start(f32[128]{0:T(128)} %param.16) | copy-start | bytes 1540
  53.5 139.7 %all-gather.2.cloned.1.call-start = ((), (), s32[]{:S(2)}) async-start(), calls=%async_computation.3 | async-start | bytes 17694720 | tf_op jit(solution)/shard_map/all_gather | solution.py:121
  89.2 47.8 %all-to-all-start = ((bf16[4,2,2560]{2,1,0:T(2,128)(2,1)}), bf16[4,2,2560]{2,1,0:T(2,128)(2,1)}, u32[]{:S(2)}, u32[]{:S(2)}) async-start(bf16[4,2,2560]{2,1,0:T(2,128)(2,1)} %reshape.193), calls=%async_computation.1 | async-start | bytes 81920 | tf_op jit(solution)/shard_map/all_to_all | solution.py:108
  139.5 0.6 copy-start.7
  143.5 0.7 copy-start.2
  146.0 10.0 %collective-permute-start.2 = (bf16[3,1,80,512]{3,2,1,0:T(8,128)(2,1)}, bf16[3,1,80,512]{3,2,1,0:T(8,128)(2,1)}, u32[]{:S(2)}, u32[]{:S(2)}) collective-permute-start(bf16[3,1,80,512]{3,2,1,0:T(8,128)(2,1)} %get-tuple-element.41), channel_id=1, source_target_pairs={{0,4},{4,8},{8,12},{12,16},{16,20},{20,24},{24,28},{1,5},{5,9},{9,... | collective-permute-start | bytes 737288 | tf_op jit(solution)/shard_map/ppermute | solution.py:21
  148.3 14.0 %collective-permute-start.3 = (bf16[3,1,80,512]{3,2,1,0:T(8,128)(2,1)}, bf16[3,1,80,512]{3,2,1,0:T(8,128)(2,1)}, u32[]{:S(2)}, u32[]{:S(2)}) collective-permute-start(bf16[3,1,80,512]{3,2,1,0:T(8,128)(2,1)} %get-tuple-element.42), channel_id=1, source_target_pairs={{4,0},{8,4},{12,8},{16,12},{20,16},{24,20},{28,24},{5,1},{9,5},{13... | collective-permute-start | bytes 737288 | tf_op jit(solution)/shard_map/ppermute | solution.py:23
  155.8 16.0 %copy-start.1 = (bf16[2,2,80,512]{3,2,1,0:T(8,128)(2,1)S(1)}, bf16[2,2,80,512]{3,2,1,0:T(8,128)(2,1)}, u32[]{:S(2)}) copy-start(bf16[2,2,80,512]{3,2,1,0:T(8,128)(2,1)} %param.17) | copy-start | bytes 983044
  155.8 16.0 %copy-start.3 = (bf16[1,2,80,512]{3,2,1,0:T(8,128)(2,1)S(1)}, bf16[1,2,80,512]{3,2,1,0:T(8,128)(2,1)}, u32[]{:S(2)}) copy-start(bf16[1,2,80,512]{3,2,1,0:T(8,128)(2,1)} %copy-done.2) | copy-start | bytes 491524
  163.2 5.9 %collective-permute-start.4 = (bf16[3,4,1,512]{3,2,1,0:T(2,128)(2,1)S(1)}, bf16[3,4,1,512]{3,2,1,0:T(2,128)(2,1)S(1)}, u32[]{:S(2)}, u32[]{:S(2)}) collective-permute-start(bf16[3,4,1,512]{3,2,1,0:T(2,128)(2,1)S(1)} %get-tuple-element.31), channel_id=1, source_target_pairs={{0,1},{1,2},{2,3},{4,5},{5,6},{6,7},{8,9},{9,10},{10,11},{12,13},{... | collective-permute-start | bytes 36872 | tf_op jit(solution)/shard_map/ppermute | solution.py:21
  165.8 6.0 %collective-permute-start.5 = (bf16[3,4,1,512]{3,2,1,0:T(2,128)(2,1)S(1)}, bf16[3,4,1,512]{3,2,1,0:T(2,128)(2,1)S(1)}, u32[]{:S(2)}, u32[]{:S(2)}) collective-permute-start(bf16[3,4,1,512]{3,2,1,0:T(2,128)(2,1)S(1)} %get-tuple-element.30), channel_id=1, source_target_pairs={{1,0},{2,1},{3,2},{5,4},{6,5},{7,6},{9,8},{10,9},{11,10},{13,12},{... | collective-permute-start | bytes 36872 | tf_op jit(solution)/shard_map/ppermute | solution.py:23
  173.6 3.2 %slice-start = ((bf16[2,2,80,512]{3,2,1,0:T(8,128)(2,1)}), bf16[1,2,80,512]{3,2,1,0:T(8,128)(2,1)S(1)}, s32[]{:S(2)}) async-start(bf16[2,2,80,512]{3,2,1,0:T(8,128)(2,1)} %param.17), calls=%async_computation.4 | async-start | bytes 327680 | tf_op jit(solution)/shard_map/slice | solution.py:36
  180.3 9.2 %copy-start.4 = (f32[160,512]{1,0:T(8,128)S(1)}, f32[160,512]{1,0:T(8,128)}, u32[]{:S(2)}) copy-start(f32[160,512]{1,0:T(8,128)} %convert_element_type.70) | copy-start | bytes 983044
  180.3 9.2 %copy-start.8 = (f32[512]{0:T(512)S(1)}, f32[512]{0:T(512)}, u32[]{:S(2)}) copy-start(f32[512]{0:T(512)} %mul.120) | copy-start | bytes 6148
  180.3 9.2 %copy-start.9 = (f32[512]{0:T(512)S(1)}, f32[512]{0:T(512)}, u32[]{:S(2)}) copy-start(f32[512]{0:T(512)} %sub.48) | copy-start | bytes 6148
  180.3 9.2 %copy-start.10 = (f32[512]{0:T(512)S(1)}, f32[512]{0:T(512)}, u32[]{:S(2)}) copy-start(f32[512]{0:T(512)} %param.19) | copy-start | bytes 6148
  180.3 9.2 %copy-start.11 = (f32[512]{0:T(512)S(1)}, f32[512]{0:T(512)}, u32[]{:S(2)}) copy-start(f32[512]{0:T(512)} %param.18) | copy-start | bytes 6148
  183.9 9.3 %copy-start.12 = (f32[512]{0:T(512)S(1)}, f32[512]{0:T(512)}, u32[]{:S(2)}) copy-start(f32[512]{0:T(512)} %param.21) | copy-start | bytes 6148
Sparse Core Ops, SparseCore 0:
  53.6 28.8 reduce-scatter.1
  84.1 95.1 all-gather.1
where the time goes:
time: 211 us; the launch traced here: 210 us
  blocking collectives  69.4 us (33%)
  waiting for transfers between devices  40 us (19%)
  local copies, waits for them, and re-layouts  34.6 us (16%)
  starting transfers between devices  23.2 us (11%)
  other arithmetic  17.6 us (8%)
  between operations  13.8 us (7%)
  matrix products  11 us (5%)
    psum x1, blocking collectives, on_device(): lax.psum((place(own_sum), place(jnp.sum(merged_groups * merged_groups, ax...  40.6 us
    reduce_scatter x1, waiting for transfers between devices, on_device(): lax.psum_scatter(lax.dot_general(kernel, columns, (((0,), (1,)), ((), ())...  28.3 us
    unnamed x86, local copies, waits for them, and re-layouts  23.5 us
    psum x1, blocking collectives, on_device(): lax.psum(jnp.sum(grouped, axis=(0, 1, 2, 4)), 'space') / entries  15.1 us
    psum x1, blocking collectives, on_device(): lax.psum(jnp.sum(centred * centred, axis=(0, 1, 2, 4)), 'space') / entries  13.7 us
    ppermute x3, waiting for transfers between devices, extended(): lax.ppermute(head, axis, [((i + 1) % count, i) for i in range(ends)])  10.4 us
    ppermute x3, starting transfers between devices, extended(): lax.ppermute(head, axis, [((i + 1) % count, i) for i in range(ends)])  10.2 us
    dot_general x1, matrix products, on_device(): jnp.dot(up_columns, lax.all_gather(kernel_up, 'chan', axis=1, tiled=True)...  9.49 us
  transfers between devices with their start and end apart: 9, of which 6 were waited for; matrix products, arithmetic and copies ran while one was open for 21% of the time, Pallas kernels for 0%

commit v1 on v0

--- a/solution.py
+++ b/solution.py
@@ -1,5 +1,9 @@
+import functools
+
 import jax
 import jax.numpy as jnp
+from jax.experimental import pallas as pl
+from jax.experimental.pallas import tpu as pltpu
 from jax import lax
 from jax.sharding import PartitionSpec as P
 
@@ -125,6 +129,540 @@
     return result
 
 
+MESH = pl.DeviceIdType.MESH
+F32 = jnp.float32
+BF16 = jnp.bfloat16
+
+
+def group_total(row):
+    lane = lax.broadcasted_iota(jnp.int32, row.shape, 1)
+    width = row.shape[1]
+    step = 1
+    while step < GS:
+        upper = pltpu.roll(row, width - step, 1)
+        lower = pltpu.roll(row, step, 1)
+        row = row + jnp.where(lane % (2 * step) < step, upper, lower)
+        step *= 2
+    return row
+
+
+def local_stats(values):
+    count = values.shape[0] * GS
+    mean = group_total(jnp.sum(values, axis=0, keepdims=True)) / count
+    centred = values - mean
+    return mean, group_total(jnp.sum(centred * centred, axis=0, keepdims=True))
+
+
+def whole_stats(stats_ref, count):
+    parts = stats_ref.shape[0]
+    means = stats_ref[:, 0:1, :]
+    mean = jnp.sum(means, axis=0) / parts
+    apart = means - mean[None]
+    spread = jnp.sum(stats_ref[:, 1:2, :], axis=0) + count * jnp.sum(apart * apart, axis=0)
+    return mean, lax.rsqrt(spread / (count * parts) + epsilon)
+
+
+def norm_silu(values, mean, scale, gain, bias):
+    moved = (values - mean) * scale * gain + bias
+    shrunk = jnp.exp(-jnp.abs(moved))
+    return (moved * jnp.where(moved < 0, shrunk, 1.0) / (1.0 + shrunk)).astype(BF16)
+
+
+def from_left(values):
+    place = lax.broadcasted_iota(jnp.int32, values.shape, 0)
+    return jnp.where(place == 0, 0.0, pltpu.roll(values, 1, 0))
+
+
+def from_right(values):
+    size = values.shape[0]
+    place = lax.broadcasted_iota(jnp.int32, values.shape, 0)
+    return jnp.where(place == size - 1, 0.0, pltpu.roll(values, size - 1, 0))
+
+
+def dot(a, b):
+    return jnp.dot(a, b, preferred_element_type=F32)
+
+
+def decoder_kernel(
+    rows,
+    chans,
+    latent,
+    cache_mid,
+    gain1,
+    bias1,
+    w1_hbm,
+    conv1_bias,
+    cache_up,
+    gain2,
+    bias2,
+    w2_hbm,
+    conv2_bias,
+    out,
+    w1,
+    w2,
+    halo_mid,
+    stats1,
+    stats2,
+    part,
+    summands,
+    gathered,
+    taps,
+    rim_out,
+    rim_in,
+    normed,
+    final,
+    raised,
+    upper_cells,
+    lower_cells,
+    out_send,
+    out_recv,
+    load_sem,
+    halo_send,
+    halo_recv,
+    stat_send,
+    stat_recv,
+    sum_send,
+    sum_recv,
+    cache_send,
+    cache_recv,
+    rim_send,
+    rim_recv,
+    norm_send,
+    norm_recv,
+    last_send,
+    last_recv,
+):
+    breadth, chan_here = latent.shape
+    r = lax.axis_index("space")
+    c = lax.axis_index("chan")
+    has = (r > 0, r < rows - 1)
+    beside = (r - 1, r + 1)
+    mate = c + 1 - 2 * (c % 2)
+    across = (c + 2) % chans
+
+    def remote(src, dst, send, recv, **where):
+        return pltpu.make_async_remote_copy(
+            src_ref=src,
+            dst_ref=dst,
+            send_sem=send,
+            recv_sem=recv,
+            device_id=where,
+            device_id_type=MESH,
+        )
+
+    load1 = pltpu.make_async_copy(w1_hbm, w1, load_sem.at[0])
+    load2 = pltpu.make_async_copy(w2_hbm, w2, load_sem.at[1])
+    load1.start()
+    load2.start()
+
+    barrier = pltpu.get_barrier_semaphore()
+    for k in range(1, rows):
+        pl.semaphore_signal(
+            barrier, inc=1, device_id={"space": (r + k) % rows}, device_id_type=MESH
+        )
+    for k in range(1, chans):
+        pl.semaphore_signal(
+            barrier, inc=1, device_id={"chan": (c + k) % chans}, device_id_type=MESH
+        )
+    for side in range(2):
+
+        @pl.when(has[side])
+        def _():
+            for k in range(1, chans):
+                pl.semaphore_signal(
+                    barrier,
+                    inc=1,
+                    device_id={"space": beside[side], "chan": (c + k) % chans},
+                    device_id_type=MESH,
+                )
+
+    values = latent[...].astype(F32)
+    mean, spread = local_stats(values)
+    stats1[0, 0:1, :] = mean
+    stats1[0, 1:2, :] = spread
+    taps[...] = jnp.zeros_like(taps)
+    for side in range(2):
+
+        @pl.when(jnp.logical_not(has[side]))
+        def _():
+            halo_mid[side] = jnp.zeros(halo_mid.shape[1:], BF16)
+            rim_in[side] = jnp.zeros(rim_in.shape[1:], F32)
+            normed[2 * side] = jnp.zeros(normed.shape[1:], BF16)
+
+    sides = has[0].astype(jnp.int32) + has[1].astype(jnp.int32)
+    pl.semaphore_wait(barrier, rows - 1 + (chans - 1) * (1 + sides))
+
+    def share(stats, which):
+        copies = []
+        for k in range(1, rows):
+            copy = remote(
+                stats.at[0],
+                stats.at[k],
+                stat_send.at[which, k],
+                stat_recv.at[which, k],
+                space=(r + k) % rows,
+            )
+            copy.start()
+            copies.append(copy)
+        return copies
+
+    first_stats = share(stats1, 0)
+
+    def halo_copies(side):
+        return (
+            remote(
+                cache_mid,
+                halo_mid.at[1 - side, pl.ds(0, 2)],
+                halo_send.at[side, 0],
+                halo_recv.at[1 - side, 0],
+                space=beside[side],
+            ),
+            remote(
+                latent,
+                halo_mid.at[1 - side, 2],
+                halo_send.at[side, 1],
+                halo_recv.at[1 - side, 1],
+                space=beside[side],
+            ),
+        )
+
+    def halo_arrivals(side):
+        return (
+            remote(
+                cache_mid,
+                halo_mid.at[side, pl.ds(0, 2)],
+                halo_send.at[side, 0],
+                halo_recv.at[side, 0],
+                space=beside[side],
+            ),
+            remote(
+                latent,
+                halo_mid.at[side, 2],
+                halo_send.at[side, 1],
+                halo_recv.at[side, 1],
+                space=beside[side],
+            ),
+        )
+
+    for side in range(2):
+
+        @pl.when(has[side])
+        def _():
+            for copy in halo_copies(side):
+                copy.start()
+
+    own_across = remote(
+        cache_up, gathered.at[c], cache_send.at[0], cache_recv.at[0], chan=across
+    )
+    own_mate = remote(cache_up, gathered.at[c], cache_send.at[1], cache_recv.at[1], chan=mate)
+    passed = remote(
+        gathered.at[across], gathered.at[across], cache_send.at[2], cache_recv.at[2], chan=mate
+    )
+    own_across.start()
+    own_mate.start()
+    gathered[c] = cache_up[...]
+
+    for side in range(2):
+
+        @pl.when(has[side])
+        def _():
+            for copy in halo_arrivals(side):
+                copy.wait_recv()
+
+    def mid_taps(pieces, frames):
+        cells = jnp.concatenate(pieces, axis=1)
+        products = []
+        for dx in range(3):
+            weights = w1[frames, :, dx].reshape(cells.shape[1], w1.shape[-1])
+            products.append(dot(cells, weights))
+        return from_left(products[0]) + products[1] + from_right(products[2])
+
+    load1.wait()
+    pieces = []
+    for frame in range(2):
+        pieces += [halo_mid[0, frame], cache_mid[frame], halo_mid[1, frame]]
+    cached_mid = mid_taps(pieces, slice(0, 2))
+
+    for copy in first_stats:
+        copy.wait_recv()
+    mean, scale = whole_stats(stats1, breadth * GS)
+    pieces = []
+    for side in range(2):
+        rim = norm_silu(halo_mid[side, 2].astype(F32), mean, scale, gain1[...], bias1[...])
+        pieces.append(jnp.where(has[side], rim.astype(F32), 0.0).astype(BF16))
+    pieces.insert(1, norm_silu(values, mean, scale, gain1[...], bias1[...]))
+    partial = cached_mid + mid_taps(pieces, slice(2, 3))
+    for block in range(chans):
+        part[block] = partial[:, block * chan_here : (block + 1) * chan_here]
+    sums = []
+    for k in (2, 3, 1):
+        to = (c + k) % chans
+        copy = remote(part.at[to], summands.at[c], sum_send.at[k], sum_recv.at[k], chan=to)
+        copy.start()
+        sums.append(copy)
+    summands[c] = part[c]
+
+    def up_taps(base):
+        def step(index, _):
+            frame = index // 3
+            dy = index % 3
+            cells = gathered[pl.ds(base, 2), frame]
+            cells = cells.reshape(-1, cells.shape[-1])
+            weights = jnp.concatenate([w2[frame, dy, dx] for dx in range(3)], axis=1)
+            product = dot(cells, weights).reshape((2, 2) + taps.shape[2:])
+            for row in range(2):
+                taps[row + 2 - dy, pl.ds(base, 2)] += product[:, row]
+            return 0
+
+        lax.fori_loop(0, 6, step, 0)
+
+    base = c - c % 2
+    load2.wait()
+    own_mate.wait_recv()
+    up_taps(base)
+    own_across.wait_recv()
+    passed.start()
+
+    for copy in sums:
+        copy.wait_recv()
+    conv_mid = summands[0]
+    for block in range(1, chans):
+        conv_mid = conv_mid + summands[block]
+    merged = (values + conv_mid + conv1_bias[...]).astype(BF16).astype(F32)
+    mean, spread = local_stats(merged)
+    stats2[0, 0:1, :] = mean
+    stats2[0, 1:2, :] = spread
+    second_stats = share(stats2, 1)
+
+    passed.wait_recv()
+    up_taps((base + 2) % chans)
+
+    def combined(row):
+        cells = taps[row].reshape(-1, taps.shape[-1])
+        lanes = [cells[:, dx * chan_here : (dx + 1) * chan_here] for dx in range(3)]
+        return from_left(lanes[0]) + lanes[1] + from_right(lanes[2])
+
+    for side in range(2):
+        rim_out[side] = combined(3 * side)
+        final[side] = combined(1 + side) + conv2_bias[c]
+
+    for copy in second_stats:
+        copy.wait_recv()
+    mean, scale = whole_stats(stats2, breadth * GS)
+    normed[1, c] = norm_silu(merged, mean, scale, gain2[c], bias2[c])
+
+    def spread_normed(row, k, **where):
+        return remote(
+            normed.at[1, c], normed.at[row, c], norm_send.at[row, k], norm_recv.at[row, k], **where
+        )
+
+    def rim_copy(side):
+        return remote(
+            rim_out.at[side],
+            rim_in.at[1 - side],
+            rim_send.at[side],
+            rim_recv.at[1 - side],
+            space=beside[side],
+        )
+
+    def rim_arrival(side):
+        return remote(
+            rim_out.at[side],
+            rim_in.at[side],
+            rim_send.at[side],
+            rim_recv.at[side],
+            space=beside[side],
+        )
+
+    along = []
+    for k in (2, 3, 1):
+        copy = spread_normed(1, k, chan=(c + k) % chans)
+        copy.start()
+        along.append(copy)
+
+    def to_side(side, k):
+        return spread_normed(
+            2 * (1 - side), k, space=beside[side], chan=(c + k) % chans
+        )
+
+    for k in (2, 3, 1, 0):
+        for side in range(2):
+
+            @pl.when(has[side])
+            def _():
+                to_side(side, k).start()
+
+    for side in range(2):
+
+        @pl.when(has[side])
+        def _():
+            rim_copy(side).start()
+
+    def raise_taps(row, dy, slot):
+        cells = jnp.concatenate([normed[row, block] for block in range(chans)], axis=1)
+        weights = jnp.concatenate([w2[2, dy, dx] for dx in range(3)], axis=1)
+        raised[slot] = dot(cells, weights)
+
+    def raise_centre(dy, _):
+        raise_taps(1, dy, dy)
+        return 0
+
+    def raise_rim(side, _):
+        raise_taps(2 * side, 2 * side, 3 + side)
+        return 0
+
+    for copy in along:
+        copy.wait_recv()
+    lax.fori_loop(0, 3, raise_centre, 0)
+
+    for side in range(2):
+
+        @pl.when(has[side])
+        def _():
+            for k in range(chans):
+                spread_normed(2 * side, k, space=beside[side], chan=c).wait_recv()
+
+    lax.fori_loop(0, 2, raise_rim, 0)
+
+    for side in range(2):
+
+        @pl.when(has[side])
+        def _():
+            rim_arrival(side).wait_recv()
+
+    for row in range(2):
+        product = raised[1] + raised[2 * (1 - row)] + raised[3 + row]
+        lanes = [product[:, dx * chan_here : (dx + 1) * chan_here] for dx in range(3)]
+        even = from_left(lanes[0]) + lanes[1] + lanes[2]
+        odd = lanes[0] + lanes[1] + from_right(lanes[2])
+        woven = (upper_cells, lower_cells)[row]
+        woven[pl.ds(0, breadth, stride=2), :] = even
+        woven[pl.ds(1, breadth, stride=2), :] = odd
+        result = (final[row] + rim_in[row] + woven[...]).astype(BF16)
+        share_cols = out.shape[1]
+        for block in range(chans):
+            out_send[block, row] = result[block * share_cols : (block + 1) * share_cols]
+
+    lasts = []
+    for k in (2, 3, 1):
+        to = (c + k) % chans
+        copy = remote(out_send.at[to], out_recv.at[c], last_send.at[k], last_recv.at[k], chan=to)
+        copy.start()
+        lasts.append(copy)
+    out_recv[c] = out_send[c]
+
+    for copy in first_stats + second_stats + sums + along + [own_across, own_mate, passed]:
+        copy.wait_send()
+    for side in range(2):
+
+        @pl.when(has[side])
+        def _():
+            for copy in halo_copies(side):
+                copy.wait_send()
+            for k in range(chans):
+                to_side(side, k).wait_send()
+            rim_copy(side).wait_send()
+
+    for copy in lasts:
+        copy.wait_recv()
+    for block in range(chans):
+        out[:, :, block * chan_here : (block + 1) * chan_here] = out_recv[block]
+    for copy in lasts:
+        copy.wait_send()
+
+
+def fused_on_device(
+    rows,
+    chans,
+    latent,
+    cache_mid,
+    norm1_gain,
+    norm1_bias,
+    conv1_weight,
+    conv1_bias,
+    cache_up,
+    norm2_gain,
+    norm2_bias,
+    conv2_weight,
+    conv2_bias,
+):
+    breadth, chan_here = latent.shape[2:]
+    up_rows, up_cols, chan_all = cache_up.shape[1:]
+    vmem = pl.BlockSpec(memory_space=pltpu.VMEM)
+    hbm = pl.BlockSpec(memory_space=pl.ANY)
+    dma = pltpu.SemaphoreType.DMA
+    result = pl.pallas_call(
+        functools.partial(decoder_kernel, rows, chans),
+        out_shape=jax.ShapeDtypeStruct((up_rows, up_cols, chan_all), BF16),
+        in_specs=[vmem, vmem, vmem, vmem, hbm, vmem, vmem, vmem, vmem, hbm, vmem],
+        out_specs=vmem,
+        scratch_shapes=[
+            pltpu.VMEM(conv1_weight.shape, BF16),
+            pltpu.VMEM(conv2_weight.shape, BF16),
+            pltpu.VMEM((2, 3, breadth, chan_here), BF16),
+            pltpu.VMEM((rows, 8, chan_here), F32),
+            pltpu.VMEM((rows, 8, chan_here), F32),
+            pltpu.VMEM((chans, breadth, chan_here), F32),
+            pltpu.VMEM((chans, breadth, chan_here), F32),
+            pltpu.VMEM((chans,) + cache_up.shape, BF16),
+            pltpu.VMEM((4, chans, up_cols, 3 * chan_here), F32),
+            pltpu.VMEM((2, 2 * breadth, chan_here), F32),
+            pltpu.VMEM((2, 2 * breadth, chan_here), F32),
+            pltpu.VMEM((3, chans, breadth, chan_here), BF16),
+            pltpu.VMEM((2, 2 * breadth, chan_here), F32),
+            pltpu.VMEM((5, breadth, 3 * chan_here), F32),
+            pltpu.VMEM((2 * breadth, chan_here), F32),
+            pltpu.VMEM((2 * breadth, chan_here), F32),
+            pltpu.VMEM((chans, up_rows, up_cols, chan_here), BF16),
+            pltpu.VMEM((chans, up_rows, up_cols, chan_here), BF16),
+            dma((2,)),
+            dma((2, 2)),
+            dma((2, 2)),
+            dma((2, rows)),
+            dma((2, rows)),
+            dma((chans,)),
+            dma((chans,)),
+            dma((3,)),
+            dma((3,)),
+            dma((2,)),
+            dma((2,)),
+            dma((3, chans)),
+            dma((3, chans)),
+            dma((chans,)),
+            dma((chans,)),
+        ],
+        compiler_params=pltpu.CompilerParams(
+            collective_id=0, has_side_effects=True, vmem_limit_bytes=48 * 2**20
+        ),
+    )(
+        latent[0, 0],
+        cache_mid[:, 0],
+        norm1_gain[None],
+        norm1_bias[None],
+        conv1_weight,
+        conv1_bias[None],
+        cache_up,
+        norm2_gain.reshape(chans, 1, chan_here),
+        norm2_bias.reshape(chans, 1, chan_here),
+        conv2_weight,
+        conv2_bias.reshape(chans, 1, chan_here),
+    )
+    return result[None]
+
+
+def fits_kernel(
+    rows, chans, latent, cache_up
+):
+    return (
+        latent.shape[:2] == (1, 1)
+        and cache_up.shape[:2] == (2, 2)
+        and chans == 4
+        and rows > 1
+        and latent.shape[3] == 128
+        and cache_up.shape[2] % 16 == 0
+    )
+
+
 def solution(mesh):
     placed = (
         P(None, "space", None, "chan"),
@@ -139,8 +677,16 @@
         P(None, None, None, None, "chan"),
         P(),
     )
+    rows = mesh.shape["space"]
+    chans = mesh.shape["chan"]
+
+    def one_device(*args):
+        if fits_kernel(rows, chans, args[0], args[6]):
+            return fused_on_device(rows, chans, *args)
+        return on_device(*args)
+
     return jax.shard_map(
-        on_device,
+        one_device,
         mesh=mesh,
         in_specs=placed,
         out_specs=P(None, "space", "chan", None),

time: 211 us -> 51.1 us (0.24)
  blocking collectives: 69.4 us -> 0 us
  Pallas kernels: 0 us -> 41.4 us
  waiting for transfers between devices: 40 us -> 0 us
  local copies, waits for them, and re-layouts: 34.6 us -> 9.31 us
  starting transfers between devices: 23.2 us -> 0 us
  other arithmetic: 17.6 us -> 0 us
  between operations: 13.8 us -> 0.02 us
  matrix products: 11 us -> 0 us
    psum x3 -> x0, blocking collectives: 69.4 us -> none  [the longest x1 40.6 us: on_device(): lax.psum((place(own_sum), place(jnp.sum(merged_groups * merged_groups, ax...]
    pallas_call x0 -> x1, Pallas kernels: none -> 41.4 us  [fused_on_device(): pl.pallas_call(functools.partial(decoder_kernel, rows, chans), out_shape=...]
    reduce_scatter x1 -> x0, waiting for transfers between devices: 28.3 us -> none  [on_device(): lax.psum_scatter(lax.dot_general(kernel, columns, (((0,), (1,)), ((), ())...]
    ppermute x6 -> x0, starting transfers between devices: 18.6 us -> none  [the longest x3 10.2 us: extended(): lax.ppermute(head, axis, [((i + 1) % count, i) for i in range(ends)])]
    unnamed x86 -> x21, local copies, waits for them, and re-layouts: 23.5 us -> 9.31 us
    ppermute x6 -> x0, waiting for transfers between devices: 11 us -> none  [the longest x3 10.4 us: extended(): lax.ppermute(head, axis, [((i + 1) % count, i) for i in range(ends)])]
    dot_general x2 -> x0, matrix products: 11 us -> none  [the longest x1 9.49 us: on_device(): jnp.dot(up_columns, lax.all_gather(kernel_up, 'chan', axis=1, tiled=True)...]
    concatenate x6 -> x0, other arithmetic: 7.83 us -> none  [the longest x4 5.09 us: extended(): jnp.concatenate([lax.ppermute(tail, axis, [(i, (i + 1) % count) for i in...]
  transfers between devices with their start and end apart: 9 -> 0, of which waited for: 6 -> 0; matrix products, arithmetic and copies ran while one was open for 21% -> 0% of each run, Pallas kernels for 0% -> 0%
where the time goes in v1:
time: 51.1 us; the launch traced here: 50.7 us
  Pallas kernels  41.4 us (81%)
  local copies, waits for them, and re-layouts  9.31 us (18%)
    pallas_call x1, Pallas kernels, fused_on_device(): pl.pallas_call(functools.partial(decoder_kernel, rows, chans), out_shape=...  41.4 us
    unnamed x21, local copies, waits for them, and re-layouts  9.31 us

profile of v1, /device:TPU:9, one launch (start us, length us, event | category | flops | bytes accessed | tf_op | source)
XLA Modules:
  0.0 50.7 jit_solution(12993975380824116143)
XLA Ops:
  0.0 0.0 copy-start
  0.0 2.0 %copy-done = bf16[3,3,3,128,512]{4,3,2,1,0:T(8,128)(2,1)S(1)} copy-done((bf16[3,3,3,128,512]{4,3,2,1,0:T(8,128)(2,1)S(1)}, bf16[3,3,3,128,512]{4,3,2,1,0:T(8,128)(2,1)}, u32[]{:S(2)}) %copy-start) | copy-done | bytes 3538968
  2.0 0.0 copy-start.1
  2.0 1.0 %copy-done.1 = bf16[2,2,80,512]{3,2,1,0:T(8,128)(2,1)S(1)} copy-done((bf16[2,2,80,512]{3,2,1,0:T(8,128)(2,1)S(1)}, bf16[2,2,80,512]{3,2,1,0:T(8,128)(2,1)}, u32[]{:S(2)}) %copy-start.1) | copy-done | bytes 327704
  3.0 0.0 copy-start.2
  3.0 0.9 %copy-done.2 = bf16[2,1,160,128]{3,2,1,0:T(8,128)(2,1)S(1)} copy-done((bf16[2,1,160,128]{3,2,1,0:T(8,128)(2,1)S(1)}, bf16[2,1,160,128]{3,2,1,0:T(8,128)(2,1)}, u32[]{:S(2)}) %copy-start.2) | copy-done | bytes 81944
  3.9 0.0 copy-start.3
  3.9 0.8 %copy-done.3 = bf16[1,1,160,128]{3,2,1,0:T(8,128)(2,1)S(1)} copy-done((bf16[1,1,160,128]{3,2,1,0:T(8,128)(2,1)S(1)}, bf16[1,1,160,128]{3,2,1,0:T(8,128)(2,1)}, u32[]{:S(2)}) %copy-start.3) | copy-done | bytes 40984
  4.6 0.0 copy-start.4
  4.6 0.7 %copy-done.4 = f32[512]{0:T(512)S(1)} copy-done((f32[512]{0:T(512)S(1)}, f32[512]{0:T(512)}, u32[]{:S(2)}) %copy-start.4) | copy-done | bytes 2072
  5.3 0.0 copy-start.5
  5.3 0.7 %copy-done.5 = f32[512]{0:T(512)S(1)} copy-done((f32[512]{0:T(512)S(1)}, f32[512]{0:T(512)}, u32[]{:S(2)}) %copy-start.5) | copy-done | bytes 2072
  6.0 0.0 copy-start.6
  6.0 0.7 %copy-done.6 = f32[512]{0:T(512)S(1)} copy-done((f32[512]{0:T(512)S(1)}, f32[512]{0:T(512)}, u32[]{:S(2)}) %copy-start.6) | copy-done | bytes 2072
  6.7 0.0 copy-start.7
  6.7 0.7 %copy-done.7 = f32[128]{0:T(128)S(1)} copy-done((f32[128]{0:T(128)S(1)}, f32[128]{0:T(128)}, u32[]{:S(2)}) %copy-start.7) | copy-done | bytes 536
  7.3 0.0 copy-start.8
  7.3 0.7 %copy-done.8 = f32[128]{0:T(128)S(1)} copy-done((f32[128]{0:T(128)S(1)}, f32[128]{0:T(128)}, u32[]{:S(2)}) %copy-start.8) | copy-done | bytes 536
  8.0 0.0 copy-start.9
  8.0 0.7 %copy-done.9 = f32[128]{0:T(128)S(1)} copy-done((f32[128]{0:T(128)S(1)}, f32[128]{0:T(128)}, u32[]{:S(2)}) %copy-start.9) | copy-done | bytes 536
  8.7 41.4 %shard_map.109 = bf16[2,80,512]{2,1,0:T(8,128)(2,1)S(1)} custom-call(bf16[160,128]{1,0:T(8,128)(2,1)S(1)} %bitcast.11, bf16[2,160,128]{2,1,0:T(8,128)(2,1)S(1)} %bitcast.10, f32[1,128]{1,0:T(1,128)S(1)} %bitcast.15, f32[1,128]{1,0:T(1,128)S(1)} %bitcast.16, bf16[3,3,3,128,512]{4,3,2,1,0:T(8,128)(2,1)S(1)} %copy-done, f32[1,128]{1,0:T(1,128)S(1)} %bitcast.17, ...), custom_call_target="tpu_custom_call" | custom-call | tf_op jit(solution)/shard_map/pallas_call | solution.py:594
  50.1 0.7 %copy.13 = bf16[1,2,80,512]{3,2,1,0:T(8,128)(2,1)} copy(bf16[1,2,80,512]{3,2,1,0:T(8,128)(2,1)S(1)} %bitcast.9) | data formatting | bytes 327680
Async XLA Ops:
  0.0 2.0 %copy-start = (bf16[3,3,3,128,512]{4,3,2,1,0:T(8,128)(2,1)S(1)}, bf16[3,3,3,128,512]{4,3,2,1,0:T(8,128)(2,1)}, u32[]{:S(2)}) copy-start(bf16[3,3,3,128,512]{4,3,2,1,0:T(8,128)(2,1)} %w1_hbm.1) | copy-start | bytes 10616836
  2.0 1.0 %copy-start.1 = (bf16[2,2,80,512]{3,2,1,0:T(8,128)(2,1)S(1)}, bf16[2,2,80,512]{3,2,1,0:T(8,128)(2,1)}, u32[]{:S(2)}) copy-start(bf16[2,2,80,512]{3,2,1,0:T(8,128)(2,1)} %cache_up.1) | copy-start | bytes 983044
  3.0 0.9 %copy-start.2 = (bf16[2,1,160,128]{3,2,1,0:T(8,128)(2,1)S(1)}, bf16[2,1,160,128]{3,2,1,0:T(8,128)(2,1)}, u32[]{:S(2)}) copy-start(bf16[2,1,160,128]{3,2,1,0:T(8,128)(2,1)} %param.12) | copy-start | bytes 245764
  3.9 0.8 %copy-start.3 = (bf16[1,1,160,128]{3,2,1,0:T(8,128)(2,1)S(1)}, bf16[1,1,160,128]{3,2,1,0:T(8,128)(2,1)}, u32[]{:S(2)}) copy-start(bf16[1,1,160,128]{3,2,1,0:T(8,128)(2,1)} %param.11) | copy-start | bytes 122884
  4.6 0.7 %copy-start.4 = (f32[512]{0:T(512)S(1)}, f32[512]{0:T(512)}, u32[]{:S(2)}) copy-start(f32[512]{0:T(512)} %param.18) | copy-start | bytes 6148
  5.3 0.7 %copy-start.5 = (f32[512]{0:T(512)S(1)}, f32[512]{0:T(512)}, u32[]{:S(2)}) copy-start(f32[512]{0:T(512)} %param.19) | copy-start | bytes 6148
  6.0 0.7 %copy-start.6 = (f32[512]{0:T(512)S(1)}, f32[512]{0:T(512)}, u32[]{:S(2)}) copy-start(f32[512]{0:T(512)} %param.21) | copy-start | bytes 6148
  6.7 0.7 %copy-start.7 = (f32[128]{0:T(128)S(1)}, f32[128]{0:T(128)}, u32[]{:S(2)}) copy-start(f32[128]{0:T(128)} %param.13) | copy-start | bytes 1540
  7.3 0.7 %copy-start.8 = (f32[128]{0:T(128)S(1)}, f32[128]{0:T(128)}, u32[]{:S(2)}) copy-start(f32[128]{0:T(128)} %param.14) | copy-start | bytes 1540
  8.0 0.7 %copy-start.9 = (f32[128]{0:T(128)S(1)}, f32[128]{0:T(128)}, u32[]{:S(2)}) copy-start(f32[128]{0:T(128)} %param.16) | copy-start | bytes 1540

commit v2 on v1

--- a/solution.py
+++ b/solution.py
@@ -186,18 +186,26 @@
 def decoder_kernel(
     rows,
     chans,
+    latent_hbm,
+    cache_mid_hbm,
+    gain1_hbm,
+    bias1_hbm,
+    w1_hbm,
+    conv1_bias_hbm,
+    cache_up,
+    gain2_hbm,
+    bias2_hbm,
+    w2_hbm,
+    conv2_bias_hbm,
+    out,
     latent,
     cache_mid,
     gain1,
     bias1,
-    w1_hbm,
     conv1_bias,
-    cache_up,
     gain2,
     bias2,
-    w2_hbm,
     conv2_bias,
-    out,
     w1,
     w2,
     halo_mid,
@@ -214,6 +222,8 @@
     raised,
     upper_cells,
     lower_cells,
+    above_cells,
+    below_cells,
     out_send,
     out_recv,
     load_sem,
@@ -250,10 +260,25 @@
             device_id_type=MESH,
         )
 
-    load1 = pltpu.make_async_copy(w1_hbm, w1, load_sem.at[0])
-    load2 = pltpu.make_async_copy(w2_hbm, w2, load_sem.at[1])
-    load1.start()
-    load2.start()
+    moves = (
+        (latent_hbm, latent),
+        (w1_hbm, w1),
+        (cache_mid_hbm, cache_mid),
+        (gain1_hbm, gain1),
+        (bias1_hbm, bias1),
+        (conv1_bias_hbm, conv1_bias),
+        (gain2_hbm, gain2),
+        (bias2_hbm, bias2),
+        (conv2_bias_hbm, conv2_bias),
+        (cache_up, gathered.at[c]),
+        (w2_hbm, w2),
+    )
+    loads = [
+        pltpu.make_async_copy(source, target, load_sem.at[index])
+        for index, (source, target) in enumerate(moves)
+    ]
+    for load in loads:
+        load.start()
 
     barrier = pltpu.get_barrier_semaphore()
     for k in range(1, rows):
@@ -264,18 +289,7 @@
         pl.semaphore_signal(
             barrier, inc=1, device_id={"chan": (c + k) % chans}, device_id_type=MESH
         )
-    for side in range(2):
-
-        @pl.when(has[side])
-        def _():
-            for k in range(1, chans):
-                pl.semaphore_signal(
-                    barrier,
-                    inc=1,
-                    device_id={"space": beside[side], "chan": (c + k) % chans},
-                    device_id_type=MESH,
-                )
-
+    loads[0].wait()
     values = latent[...].astype(F32)
     mean, spread = local_stats(values)
     stats1[0, 0:1, :] = mean
@@ -287,10 +301,8 @@
         def _():
             halo_mid[side] = jnp.zeros(halo_mid.shape[1:], BF16)
             rim_in[side] = jnp.zeros(rim_in.shape[1:], F32)
-            normed[2 * side] = jnp.zeros(normed.shape[1:], BF16)
-
-    sides = has[0].astype(jnp.int32) + has[1].astype(jnp.int32)
-    pl.semaphore_wait(barrier, rows - 1 + (chans - 1) * (1 + sides))
+
+    pl.semaphore_wait(barrier, rows - 1 + chans - 1)
 
     def share(stats, which):
         copies = []
@@ -311,14 +323,14 @@
     def halo_copies(side):
         return (
             remote(
-                cache_mid,
+                cache_mid_hbm,
                 halo_mid.at[1 - side, pl.ds(0, 2)],
                 halo_send.at[side, 0],
                 halo_recv.at[1 - side, 0],
                 space=beside[side],
             ),
             remote(
-                latent,
+                latent_hbm,
                 halo_mid.at[1 - side, 2],
                 halo_send.at[side, 1],
                 halo_recv.at[1 - side, 1],
@@ -329,14 +341,14 @@
     def halo_arrivals(side):
         return (
             remote(
-                cache_mid,
+                cache_mid_hbm,
                 halo_mid.at[side, pl.ds(0, 2)],
                 halo_send.at[side, 0],
                 halo_recv.at[side, 0],
                 space=beside[side],
             ),
             remote(
-                latent,
+                latent_hbm,
                 halo_mid.at[side, 2],
                 halo_send.at[side, 1],
                 halo_recv.at[side, 1],
@@ -360,7 +372,8 @@
     )
     own_across.start()
     own_mate.start()
-    gathered[c] = cache_up[...]
+    for load in loads[1:-1]:
+        load.wait()
 
     for side in range(2):
 
@@ -377,7 +390,6 @@
             products.append(dot(cells, weights))
         return from_left(products[0]) + products[1] + from_right(products[2])
 
-    load1.wait()
     pieces = []
     for frame in range(2):
         pieces += [halo_mid[0, frame], cache_mid[frame], halo_mid[1, frame]]
@@ -417,7 +429,7 @@
         lax.fori_loop(0, 6, step, 0)
 
     base = c - c % 2
-    load2.wait()
+    loads[-1].wait()
     own_mate.wait_recv()
     up_taps(base)
     own_across.wait_recv()
@@ -449,12 +461,7 @@
     for copy in second_stats:
         copy.wait_recv()
     mean, scale = whole_stats(stats2, breadth * GS)
-    normed[1, c] = norm_silu(merged, mean, scale, gain2[c], bias2[c])
-
-    def spread_normed(row, k, **where):
-        return remote(
-            normed.at[1, c], normed.at[row, c], norm_send.at[row, k], norm_recv.at[row, k], **where
-        )
+    normed[c] = norm_silu(merged, mean, scale, gain2[c], bias2[c])
 
     def rim_copy(side):
         return remote(
@@ -476,53 +483,37 @@
 
     along = []
     for k in (2, 3, 1):
-        copy = spread_normed(1, k, chan=(c + k) % chans)
+        copy = remote(
+            normed.at[c], normed.at[c], norm_send.at[k], norm_recv.at[k], chan=(c + k) % chans
+        )
         copy.start()
         along.append(copy)
 
-    def to_side(side, k):
-        return spread_normed(
-            2 * (1 - side), k, space=beside[side], chan=(c + k) % chans
-        )
-
-    for k in (2, 3, 1, 0):
-        for side in range(2):
-
-            @pl.when(has[side])
-            def _():
-                to_side(side, k).start()
-
-    for side in range(2):
+    def raise_taps(dy, _):
+        cells = jnp.concatenate([normed[block] for block in range(chans)], axis=1)
+        weights = jnp.concatenate([w2[2, dy, dx] for dx in range(3)], axis=1)
+        raised[dy] = dot(cells, weights)
+        return 0
+
+    def weave(product, woven):
+        lanes = [product[:, dx * chan_here : (dx + 1) * chan_here] for dx in range(3)]
+        woven[pl.ds(0, breadth, stride=2), :] = from_left(lanes[0]) + lanes[1] + lanes[2]
+        woven[pl.ds(1, breadth, stride=2), :] = lanes[0] + lanes[1] + from_right(lanes[2])
+
+    for copy in along:
+        copy.wait_recv()
+    lax.fori_loop(0, 3, raise_taps, 0)
+    for side, woven in enumerate((above_cells, below_cells)):
+        weave(raised[2 * (1 - side)], woven)
+        rim_out[side] += woven[...]
 
         @pl.when(has[side])
         def _():
             rim_copy(side).start()
 
-    def raise_taps(row, dy, slot):
-        cells = jnp.concatenate([normed[row, block] for block in range(chans)], axis=1)
-        weights = jnp.concatenate([w2[2, dy, dx] for dx in range(3)], axis=1)
-        raised[slot] = dot(cells, weights)
-
-    def raise_centre(dy, _):
-        raise_taps(1, dy, dy)
-        return 0
-
-    def raise_rim(side, _):
-        raise_taps(2 * side, 2 * side, 3 + side)
-        return 0
-
-    for copy in along:
-        copy.wait_recv()
-    lax.fori_loop(0, 3, raise_centre, 0)
-
-    for side in range(2):
-
-        @pl.when(has[side])
-        def _():
-            for k in range(chans):
-                spread_normed(2 * side, k, space=beside[side], chan=c).wait_recv()
-
-    lax.fori_loop(0, 2, raise_rim, 0)
+    for row, woven in enumerate((upper_cells, lower_cells)):
+        weave(raised[1] + raised[2 * (1 - row)], woven)
+        final[row] += woven[...]
 
     for side in range(2):
 
@@ -531,14 +522,7 @@
             rim_arrival(side).wait_recv()
 
     for row in range(2):
-        product = raised[1] + raised[2 * (1 - row)] + raised[3 + row]
-        lanes = [product[:, dx * chan_here : (dx + 1) * chan_here] for dx in range(3)]
-        even = from_left(lanes[0]) + lanes[1] + lanes[2]
-        odd = lanes[0] + lanes[1] + from_right(lanes[2])
-        woven = (upper_cells, lower_cells)[row]
-        woven[pl.ds(0, breadth, stride=2), :] = even
-        woven[pl.ds(1, breadth, stride=2), :] = odd
-        result = (final[row] + rim_in[row] + woven[...]).astype(BF16)
+        result = (final[row] + rim_in[row]).astype(BF16)
         share_cols = out.shape[1]
         for block in range(chans):
             out_send[block, row] = result[block * share_cols : (block + 1) * share_cols]
@@ -559,8 +543,6 @@
         def _():
             for copy in halo_copies(side):
                 copy.wait_send()
-            for k in range(chans):
-                to_side(side, k).wait_send()
             rim_copy(side).wait_send()
 
     for copy in lasts:
@@ -589,14 +571,22 @@
     breadth, chan_here = latent.shape[2:]
     up_rows, up_cols, chan_all = cache_up.shape[1:]
     vmem = pl.BlockSpec(memory_space=pltpu.VMEM)
-    hbm = pl.BlockSpec(memory_space=pl.ANY)
+    hbm = pl.BlockSpec(memory_space=pltpu.HBM)
     dma = pltpu.SemaphoreType.DMA
     result = pl.pallas_call(
         functools.partial(decoder_kernel, rows, chans),
         out_shape=jax.ShapeDtypeStruct((up_rows, up_cols, chan_all), BF16),
-        in_specs=[vmem, vmem, vmem, vmem, hbm, vmem, vmem, vmem, vmem, hbm, vmem],
+        in_specs=[hbm] * 11,
         out_specs=vmem,
         scratch_shapes=[
+            pltpu.VMEM((breadth, chan_here), BF16),
+            pltpu.VMEM((2, breadth, chan_here), BF16),
+            pltpu.VMEM((1, chan_here), F32),
+            pltpu.VMEM((1, chan_here), F32),
+            pltpu.VMEM((1, chan_here), F32),
+            pltpu.VMEM((chans, 1, chan_here), F32),
+            pltpu.VMEM((chans, 1, chan_here), F32),
+            pltpu.VMEM((chans, 1, chan_here), F32),
             pltpu.VMEM(conv1_weight.shape, BF16),
             pltpu.VMEM(conv2_weight.shape, BF16),
             pltpu.VMEM((2, 3, breadth, chan_here), BF16),
@@ -608,14 +598,16 @@
             pltpu.VMEM((4, chans, up_cols, 3 * chan_here), F32),
             pltpu.VMEM((2, 2 * breadth, chan_here), F32),
             pltpu.VMEM((2, 2 * breadth, chan_here), F32),
-            pltpu.VMEM((3, chans, breadth, chan_here), BF16),
+            pltpu.VMEM((chans, breadth, chan_here), BF16),
             pltpu.VMEM((2, 2 * breadth, chan_here), F32),
-            pltpu.VMEM((5, breadth, 3 * chan_here), F32),
+            pltpu.VMEM((3, breadth, 3 * chan_here), F32),
+            pltpu.VMEM((2 * breadth, chan_here), F32),
+            pltpu.VMEM((2 * breadth, chan_here), F32),
             pltpu.VMEM((2 * breadth, chan_here), F32),
             pltpu.VMEM((2 * breadth, chan_here), F32),
             pltpu.VMEM((chans, up_rows, up_cols, chan_here), BF16),
             pltpu.VMEM((chans, up_rows, up_cols, chan_here), BF16),
-            dma((2,)),
+            dma((11,)),
             dma((2, 2)),
             dma((2, 2)),
             dma((2, rows)),
@@ -626,13 +618,13 @@
             dma((3,)),
             dma((2,)),
             dma((2,)),
-            dma((3, chans)),
-            dma((3, chans)),
+            dma((chans,)),
+            dma((chans,)),
             dma((chans,)),
             dma((chans,)),
         ],
         compiler_params=pltpu.CompilerParams(
-            collective_id=0, has_side_effects=True, vmem_limit_bytes=48 * 2**20
+            collective_id=0, has_side_effects=True, vmem_limit_bytes=56 * 2**20
         ),
     )(
         latent[0, 0],

time: 51.1 us -> 40.6 us (0.79)
  local copies, waits for them, and re-layouts: 9.31 us -> 1.59 us
  Pallas kernels: 41.4 us -> 38.8 us
    unnamed x21 -> x1, local copies, waits for them, and re-layouts: 9.31 us -> 1.59 us
    pallas_call x1, Pallas kernels: 41.4 us -> 38.8 us  [fused_on_device(): pl.pallas_call(functools.partial(decoder_kernel, rows, chans), out_shape=...]
where the time goes in v2:
time: 40.6 us; the launch traced here: 40.5 us
  Pallas kernels  38.8 us (96%)
  local copies, waits for them, and re-layouts  1.59 us (4%)
    pallas_call x1, Pallas kernels, fused_on_device(): pl.pallas_call(functools.partial(decoder_kernel, rows, chans), out_shape=...  38.8 us
    unnamed x1, local copies, waits for them, and re-layouts  1.59 us

profile of v2, /device:TPU:9, one launch (start us, length us, event | category | flops | bytes accessed | tf_op | source)
XLA Modules:
  0.0 40.5 jit_solution(15782621499043951659)
XLA Ops:
  0.0 38.8 %shard_map.109 = bf16[2,80,512]{2,1,0:T(8,128)(2,1)} custom-call(bf16[160,128]{1,0:T(8,128)(2,1)} %bitcast.11, bf16[2,160,128]{2,1,0:T(8,128)(2,1)} %bitcast.10, f32[1,128]{1,0:T(1,128)} %bitcast.15, f32[1,128]{1,0:T(1,128)} %bitcast.16, bf16[3,3,3,128,512]{4,3,2,1,0:T(8,128)(2,1)} %w1_hbm.1, f32[1,128]{1,0:T(1,128)} %bitcast.17, ...), custom_call_target="tpu_custom_call" | custom-call | tf_op jit(solution)/shard_map/pallas_call | solution.py:576
  38.9 1.6 %copy.13 = bf16[1,2,80,512]{3,2,1,0:T(8,128)(2,1)} copy(bf16[1,2,80,512]{3,2,1,0:T(8,128)(2,1)} %bitcast.9) | data formatting | bytes 327680

commit v3 on v2

--- a/solution.py
+++ b/solution.py
@@ -215,6 +215,7 @@
     summands,
     gathered,
     taps,
+    rim_sum,
     rim_out,
     rim_in,
     normed,
@@ -300,7 +301,7 @@
         @pl.when(jnp.logical_not(has[side]))
         def _():
             halo_mid[side] = jnp.zeros(halo_mid.shape[1:], BF16)
-            rim_in[side] = jnp.zeros(rim_in.shape[1:], F32)
+            rim_in[side] = jnp.zeros(rim_in.shape[1:], BF16)
 
     pl.semaphore_wait(barrier, rows - 1 + chans - 1)
 
@@ -455,7 +456,7 @@
         return from_left(lanes[0]) + lanes[1] + from_right(lanes[2])
 
     for side in range(2):
-        rim_out[side] = combined(3 * side)
+        rim_sum[side] = combined(3 * side)
         final[side] = combined(1 + side) + conv2_bias[c]
 
     for copy in second_stats:
@@ -505,7 +506,7 @@
     lax.fori_loop(0, 3, raise_taps, 0)
     for side, woven in enumerate((above_cells, below_cells)):
         weave(raised[2 * (1 - side)], woven)
-        rim_out[side] += woven[...]
+        rim_out[side] = (rim_sum[side] + woven[...]).astype(BF16)
 
         @pl.when(has[side])
         def _():
@@ -522,7 +523,7 @@
             rim_arrival(side).wait_recv()
 
     for row in range(2):
-        result = (final[row] + rim_in[row]).astype(BF16)
+        result = (final[row] + rim_in[row].astype(F32)).astype(BF16)
         share_cols = out.shape[1]
         for block in range(chans):
             out_send[block, row] = result[block * share_cols : (block + 1) * share_cols]
@@ -597,7 +598,8 @@
             pltpu.VMEM((chans,) + cache_up.shape, BF16),
             pltpu.VMEM((4, chans, up_cols, 3 * chan_here), F32),
             pltpu.VMEM((2, 2 * breadth, chan_here), F32),
-            pltpu.VMEM((2, 2 * breadth, chan_here), F32),
+            pltpu.VMEM((2, 2 * breadth, chan_here), BF16),
+            pltpu.VMEM((2, 2 * breadth, chan_here), BF16),
             pltpu.VMEM((chans, breadth, chan_here), BF16),
             pltpu.VMEM((2, 2 * breadth, chan_here), F32),
             pltpu.VMEM((3, breadth, 3 * chan_here), F32),

time: 40.6 us -> 37.3 us (0.919)
  Pallas kernels: 38.8 us -> 35.3 us
    pallas_call x1, Pallas kernels: 38.8 us -> 35.3 us  [fused_on_device(): pl.pallas_call(functools.partial(decoder_kernel, rows, chans), out_shape=...]
where the time goes in v3:
time: 37.3 us; the launch traced here: 36.9 us
  Pallas kernels  35.3 us (95%)
  local copies, waits for them, and re-layouts  1.59 us (4%)
    pallas_call x1, Pallas kernels, fused_on_device(): pl.pallas_call(functools.partial(decoder_kernel, rows, chans), out_shape=...  35.3 us
    unnamed x1, local copies, waits for them, and re-layouts  1.59 us

profile of v3, /device:TPU:9, one launch (start us, length us, event | category | flops | bytes accessed | tf_op | source)
XLA Modules:
  0.0 36.9 jit_solution(15473162631852674902)
XLA Ops:
  0.0 35.3 %shard_map.109 = bf16[2,80,512]{2,1,0:T(8,128)(2,1)} custom-call(bf16[160,128]{1,0:T(8,128)(2,1)} %bitcast.11, bf16[2,160,128]{2,1,0:T(8,128)(2,1)} %bitcast.10, f32[1,128]{1,0:T(1,128)} %bitcast.15, f32[1,128]{1,0:T(1,128)} %bitcast.16, bf16[3,3,3,128,512]{4,3,2,1,0:T(8,128)(2,1)} %w1_hbm.1, f32[1,128]{1,0:T(1,128)} %bitcast.17, ...), custom_call_target="tpu_custom_call" | custom-call | tf_op jit(solution)/shard_map/pallas_call | solution.py:577
  35.3 1.6 %copy.13 = bf16[1,2,80,512]{3,2,1,0:T(8,128)(2,1)} copy(bf16[1,2,80,512]{3,2,1,0:T(8,128)(2,1)} %bitcast.9) | data formatting | bytes 327680
